TPU v7x, 128 devices: a whole 4x4x4 slice. The times are simulated.
128 devices in a mesh: band: 16 (over x, y_hi, core), grid: 8 (over z, y_lo).
Axes of the slice: x: 4, y: 4 (y_hi: 2, y_lo: 2; y = y_hi * 2 + y_lo), z: 4, core: 2. Of those that a mesh axis runs over, the one named last changes fastest.
Arguments:
- orbitals: float32 [64, 64, 4096], P('band', 'grid'), may hold values from -6 to 6
- kernel: float32 [64, 64, 64], P(None, 'grid'), may hold values from 0.05 to 18, as said below
Outputs:
- applied: float32 [64, 64, 4096], P('band', 'grid')
Inputs may be any that keep to these rules, and one draw needn't show every extreme that they name: The kernel is even and positive: kernel[kx, ky, kz] equals kernel[(-kx) mod 64, (-ky) mod 64, (-kz) mod 64].
All inputs are finite; a program needn't handle non-finite values.
Results may differ from a plain program's by a relative error of at most 0.0003.
Values sent between devices are 32-bit elements; how exact they have to be, the bound alone decides.
A program may use at most 192 MiB of HBM per device.

v0:
```python
import math

import jax
import jax.numpy as jnp
import ml_dtypes
import numpy as np
from jax import lax
from jax.experimental import pallas as pl
from jax.experimental.pallas import tpu as pltpu
from jax.sharding import PartitionSpec as P

G = 64
BF = jnp.bfloat16
F32 = jnp.float32
H = math.sqrt(0.5)
MESH = pl.DeviceIdType.MESH
YA = 16


def split_table(matrix):
    hi = matrix.astype(ml_dtypes.bfloat16)
    return hi, (matrix - hi.astype(np.float64)).astype(ml_dtypes.bfloat16)


def tables():
    k = np.arange(G)
    angle = 2.0 * np.pi * ((k[:, None] * k[None, :]) % G) / G
    c, s = np.cos(angle), np.sin(angle)

    def left(matrix):
        hi, lo = split_table(matrix)
        return np.concatenate([hi, hi, lo], 1)

    def right(matrix):
        hi, lo = split_table(matrix)
        return np.concatenate([hi, hi, lo], 0)

    forward_x = left(np.block([[c, s], [-s, c]]))
    inverse_x = left(np.block([[c, -s], [s, c]]))
    parity = np.array([[1.0, 1.0], [1.0, -1.0]])
    cc, ss = np.kron(parity, c), np.kron(parity, s)
    forward_z = right(np.block([[cc, -ss], [ss, cc]]))
    inverse_z = right(np.block([[cc, ss], [-ss, cc]]) * (-1.0 / G**3))
    twiddle = np.ones((32, 2, 8, 128), np.float64)
    turn = 2.0 * np.pi * np.arange(32) / G
    twiddle[:, 0, :, 64:] = np.cos(turn)[:, None, None]
    twiddle[:, 1, :, :64] = 0.0
    twiddle[:, 1, :, 64:] = np.sin(turn)[:, None, None]
    return forward_x, inverse_x, forward_z, inverse_z, twiddle.astype(np.float32)


def cadd(a, b):
    return a[0] + b[0], a[1] + b[1]


def csub(a, b):
    return a[0] - b[0], a[1] - b[1]


def rot(a, sign):
    return (-a[1], a[0]) if sign > 0 else (a[1], -a[0])


def dft4(v, sign):
    p, q = cadd(v[0], v[2]), csub(v[0], v[2])
    r, t = cadd(v[1], v[3]), csub(v[1], v[3])
    t = rot(t, sign)
    return [cadd(p, r), cadd(q, t), csub(p, r), csub(q, t)]


def dft8(v, sign):
    e = dft4(v[0::2], sign)
    o = dft4(v[1::2], sign)
    a, b = o[1], o[3]
    if sign > 0:
        o[1] = (H * (a[0] - a[1]), H * (a[0] + a[1]))
        o[3] = (-H * (b[0] + b[1]), H * (b[0] - b[1]))
    else:
        o[1] = (H * (a[0] + a[1]), H * (a[1] - a[0]))
        o[3] = (H * (b[1] - b[0]), -H * (b[0] + b[1]))
    o[2] = rot(o[2], sign)
    return [cadd(e[i], o[i]) for i in range(4)] + [csub(e[i], o[i]) for i in range(4)]


def dft32(load, store, sign):
    mid = {}
    for n2 in range(4):
        out = dft8([load(4 * n1 + n2) for n1 in range(8)], sign)
        for k1 in range(8):
            v = out[k1]
            if n2 * k1 == 4:
                v = (H * (v[0] - sign * v[1]), H * (v[1] + sign * v[0]))
            elif n2 * k1:
                turn = sign * 2.0 * math.pi * n2 * k1 / 32
                c, s = math.cos(turn), math.sin(turn)
                v = (v[0] * c - v[1] * s, v[0] * s + v[1] * c)
            mid[n2, k1] = v
    for k1 in range(8):
        out = dft4([mid[n2, k1] for n2 in range(4)], sign)
        for k2 in range(4):
            store(k1 + 8 * k2, out[k2])


def split(x):
    hi = x.astype(BF)
    return hi, (x - hi.astype(F32)).astype(BF)


def dot(a, b):
    return jnp.dot(a, b, preferred_element_type=F32)


def forward_slabs(active, targ, phi, fz, tw, z, s):
    count = len(active)

    def pick(u, values):
        total, chosen, row = values[0], 1, list(values)
        for order in range(1, count):
            row = [after - before for before, after in zip(row, row[1:])]
            chosen = chosen * (u - order + 1)
            total = total + row[0] * (chosen // math.factorial(order))
        return total

    @pl.loop(0, count)
    def _(u):
        n = pick(u, [n for n, _ in active])
        slab = pick(u, [slab for _, slab in active])

        def load(y):
            at = slice(128 * y, 128 * (y + 1))
            t = targ[n, slab, :, at]
            return t * phi[0, slab, :, at], t * phi[1, slab, :, at]

        def store(k, v):
            c, w = tw[k, 0], tw[k, 1]
            s[u, k, :, 0:128] = v[0] * c + v[1] * w
            s[u, k, :, 128:256] = v[1] * c - v[0] * w

        dft32(load, store, -1)

    hi, lo = split(s[0:count].reshape(count * 256, 256))
    res = dot(jnp.concatenate([hi, lo, hi], 1), fz[...])
    for u, (n, slab) in enumerate(active):
        part = res[256 * u : 256 * (u + 1)]
        base = pl.multiple_of(8 * slab, 8)
        z[n, :, pl.ds(base, 8), :] = part[:, :128].reshape(32, 8, 128)
        z[n, :, pl.ds(64 + base, 8), :] = part[:, 128:].reshape(32, 8, 128)


def middle(n, kern, fx, ix, z):
    @pl.loop(0, 32 // YA)
    def _(step):
        ks = [step * YA + i for i in range(YA)]
        hi, lo = split(jnp.concatenate([z[n, k] for k in ks], 1))
        res = dot(fx[...], jnp.concatenate([hi, lo, hi], 0))
        kv = jnp.concatenate([kern[k] for k in ks], 1)
        hi, lo = split(res * jnp.concatenate([kv, kv], 0))
        res = dot(ix[...], jnp.concatenate([hi, lo, hi], 0))
        for i in range(YA):
            z[n, step * YA + i] = res[:, 128 * i : 128 * (i + 1)]


def inverse_slabs(n, parity, phi, iz, tw, z, s, part):
    rows = []
    for zz in range(4):
        base = pl.multiple_of(16 * zz + 8 * parity, 8)
        re = z[n, :, pl.ds(base, 8), :].reshape(256, 128)
        im = z[n, :, pl.ds(64 + base, 8), :].reshape(256, 128)
        rows.append(jnp.concatenate([re, im], 1))
    hi, lo = split(jnp.concatenate(rows, 0))
    s[...] = dot(jnp.concatenate([hi, lo, hi], 1), iz[...]).reshape(4, 32, 8, 256)

    @pl.loop(0, 4)
    def _(zz):
        slab = 2 * zz + parity

        def load(k):
            c, w = tw[k, 0], tw[k, 1]
            r, i = s[zz, k, :, 0:128], s[zz, k, :, 128:256]
            return r * c - i * w, i * c + r * w

        def store(y, v):
            at = slice(128 * y, 128 * (y + 1))
            part[zz, :, at] = v[0] * phi[0, slab, :, at] + v[1] * phi[1, slab, :, at]

        dft32(load, store, 1)


def unpack_kernel(kp, kern):
    low = lax.broadcasted_iota(jnp.int32, (64, 128), 1) < 64

    @pl.loop(0, 4)
    def _(slab):
        @pl.loop(0, 4)
        def _(r):
            a, b = kp[slab, r], kp[slab + 4, r]
            kern[slab * 8 + r] = jnp.where(low, a, pltpu.roll(b, 64, 1))
            kern[slab * 8 + 4 + r] = jnp.where(low, pltpu.roll(a, 64, 1), b)


def body(
    orb, kernel, fx_in, ix_in, fz_in, iz_in, tw_in, out,
    phi, targ, kslab, kpk, kp, kern, z, s, part, rcore, acc, fx, ix, fz, iz, tw, send, recv, local,
):
    b = lax.axis_index("band")
    q = lax.axis_index("grid")
    core, block, x = b % 2, b // 2, b // 4
    plane, ylo = q // 2, q % 2
    odd = (ylo + block) % 2
    home = (core + block) % 2
    chip = block * 2 + odd
    sibling = (block * 2 + 1 - core, q)
    near = (b, plane * 2 + 1 - ylo)
    mine = core == odd
    owner = core == plane // 2

    def device(h, c, zz):
        h = (h + 16) % 16
        return ((h // 2) * 2 + c, zz * 2 + (h + h // 2) % 2)

    def at_plane(d):
        return (b, ((plane + d) % 4) * 2 + ylo)

    def result_device(n, zz):
        return ((chip + n) % 16, zz * 2 + home)

    count = [0]

    def slots(n):
        count[0] += n
        return count[0] - n

    def remote(src, dst, s, where, r=None):
        return pltpu.make_async_remote_copy(
            src_ref=src, dst_ref=dst, send_sem=send.at[s], recv_sem=recv.at[s if r is None else r],
            device_id=where, device_id_type=MESH,
        )

    sent, sent_owner = [], []

    def start(cp):
        cp.start()
        sent.append(cp)

    loads = [
        pltpu.make_async_copy(src, dst, local.at[i])
        for i, (src, dst) in enumerate(
            [(kernel, kslab), (fx_in, fx), (ix_in, ix), (fz_in, fz), (iz_in, iz), (tw_in, tw)]
        )
    ]
    for cp in loads:
        cp.start()

    barrier = pltpu.get_barrier_semaphore()
    greeted = []
    for dc in range(2):
        for dq in range(8):
            if dc or dq:
                greeted.append(((b + dc) % 2 + block * 2, (q + dq) % 8))
    greeted.append(device(chip - 2, core, plane))
    greeted.append(device(chip + 2, core, plane))
    for n in (1, 2):
        for zz in range(4):
            greeted.append(result_device(n, zz))
            behind = (b - n + 16) % 16
            greeted.append(device(behind, (ylo + behind // 2) % 2, zz))
    for dx in (4, 8, 12):
        greeted.append(((b + dx) % 16, q))
    for where in greeted:
        pl.semaphore_signal(barrier, inc=1, device_id=where, device_id_type=MESH)
    pl.semaphore_wait(barrier, len(greeted))

    s_first = slots(4)
    firsts = {}
    for k in range(2):
        for dc in range(2):
            c = (core + dc) % 2
            src, dst = orb.at[2 * c + k], phi.at[k, q]
            firsts[dc, k] = remote(src, dst, s_first + 2 * dc + k, (block * 2 + c, plane * 2 + home), s_first + 2 * ylo + k)
    keeps = [pltpu.make_async_copy(orb.at[2 * core + k], phi.at[k, q], local.at[6 + k]) for k in range(2)]
    for k in range(2):

        @pl.when(mine)
        def _():
            keeps[k].start()

        @pl.when(jnp.logical_not(mine))
        def _():
            firsts[0, k].start()

        start(firsts[1, k])

    def wait_first(i):
        p = (ylo + i) % 2
        for k in range(2):
            piece = phi.at[k, 2 * plane + p]
            cp = remote(piece, piece, s_first, (b, q), s_first + 2 * p + k)
            if i == 0:

                @pl.when(mine)
                def _():
                    keeps[k].wait()

                @pl.when(jnp.logical_not(mine))
                def _():
                    cp.wait_recv()
            else:
                cp.wait_recv()

    s_step = slots(8)
    s_pass = slots(4)

    def slab_at(d, i):
        return ((plane + d) % 4) * 2 + (ylo + i) % 2

    def step_copy(i, side, k):
        d = (1, 3)[side]
        piece = phi.at[k, slab_at(0, i)]
        return remote(piece, piece, s_step + 4 * i + 2 * side + k, at_plane(d))

    def step_wait(i, side, k):
        piece = phi.at[k, slab_at((3, 1)[side], i)]
        remote(piece, piece, s_step, (b, q), s_step + 4 * i + 2 * side + k).wait_recv()

    def pass_copy(i, k):
        piece = phi.at[k, slab_at((3, 1)[i], i)]
        return remote(piece, piece, s_pass + 2 * i + k, at_plane((1, 3)[i]))

    def pass_wait(i, k):
        piece = phi.at[k, slab_at(2, i)]
        remote(piece, piece, s_pass, (b, q), s_pass + 2 * i + k).wait_recv()

    def step_start(i, side):
        d = (1, 3)[side]
        for turn in range(2):
            start(step_copy(i, side, (plane + d + turn) % 2))

    s_t0 = slots(8)
    s_t1 = slots(8)
    s_t2 = slots(8)
    s_t1_give = slots(8)
    s_t2_give = slots(8)
    order = [(0, 0), (3, 0), (1, 0), (0, 1), (2, 0), (1, 1), (3, 1), (2, 1)]
    kt = plane % 2
    far_back = device(chip - 2, core, plane)

    def target_slab(n, j):
        d, i = order[j]
        flip = (0, 1 - odd, 1)[n]
        return ((plane + d) % 4) * 2 + (ylo + flip + i) % 2

    def own_target(j):
        s = target_slab(0, j)
        src = phi.at[kt, s]
        keep = pltpu.make_async_copy(src, targ.at[0, s], local.at[8 + j])
        give = remote(src, targ.at[0, s], s_t0 + j, sibling)
        back = remote(src, targ.at[2, s], s_t2 + j, far_back)
        beside = remote(src, targ.at[1, s], s_t1 + j, near)
        return keep, give, back, beside

    def target_ready(j):
        @pl.when(owner)
        def _():
            keep, give, back, beside = own_target(j)
            back.start()

            @pl.when(odd == 1)
            def _():
                beside.start()

            give.start()
            keep.start()

    def far_target(j):
        s = target_slab(2, j)
        piece = targ.at[2, s]
        arrive = remote(piece, piece, s_t2, (b, q), s_t2 + j)
        beside = remote(piece, targ.at[1, s], s_t1 + j, near)
        give = remote(piece, piece, s_t2_give + j, sibling)
        return arrive, beside, give

    def far_ready(j):
        @pl.when(owner)
        def _():
            arrive, beside, give = far_target(j)
            arrive.wait_recv()

            @pl.when(odd == 0)
            def _():
                beside.start()

            give.start()

    def near_target(j):
        piece = targ.at[1, target_slab(1, j)]
        return remote(piece, piece, s_t1, (b, q), s_t1 + j), remote(piece, piece, s_t1_give + j, sibling)

    def near_ready(j):
        @pl.when(owner)
        def _():
            arrive, give = near_target(j)
            arrive.wait_recv()
            give.start()

    def wait_target(n, j):
        base = (s_t0, s_t1_give, s_t2_give)[n]

        @pl.when(jnp.logical_not(owner))
        def _():
            piece = targ.at[n, target_slab(n, j)]
            remote(piece, piece, base, (b, q), base + j).wait_recv()

        if n == 0:

            @pl.when(owner)
            def _():
                own_target(j)[0].wait()

    s_kernel = slots(11)
    kx_half = pl.ds(pl.multiple_of(32 * core, 32), 32)
    kernel_first = [
        remote(kpk.at[x, kx_half], kp.at[q, x, kx_half], s_kernel + d - 1, (b, (q + d) % 8)) for d in range(1, 8)
    ]
    kernel_second = [
        remote(kp.at[:, x, kx_half], kp.at[:, x, kx_half], s_kernel + 6 + d, ((b + 4 * d) % 16, q)) for d in (1, 3, 2)
    ]
    kernel_third = remote(kp.at[:, :, kx_half], kp.at[:, :, kx_half], s_kernel + 10, sibling)

    def pack_kernel():
        loads[0].wait()
        for r in range(4):
            kpk[r] = jnp.concatenate([kslab[:, r, :], kslab[:, r + 4, :]], 1)
        for cp in kernel_first:
            start(cp)
        kp[q, x, kx_half] = kpk[x, kx_half]

    far_steps = {3: (0,), 5: (2, 3), 6: (1,), 7: (4, 5), 8: (6,), 9: (7,)}
    near_steps = {3: (0,), 5: (2,), 6: (1, 3), 7: (4,), 8: (5,), 9: (6,), 10: (7,)}

    def forward(j):
        if 2 <= j < 10:
            far_ready(j - 2)
        if 3 <= j < 11:
            near_ready(j - 3)
        active = [(0, j)] if j < 8 else []
        active += [(2, i) for i in far_steps.get(j, ())] + [(1, i) for i in near_steps.get(j, ())]
        for n, i in active:
            wait_target(n, i)
        active = [(n, target_slab(n, i)) for n, i in active]
        forward_slabs(active, targ, phi, fz, tw, z, s)

    wait_first(0)
    step_start(0, 0)
    step_start(0, 1)
    target_ready(0)
    pack_kernel()
    for cp in loads[1:]:
        cp.wait()
    forward(0)
    step_wait(0, 0, kt)
    start(pass_copy(0, kt))
    target_ready(1)
    step_wait(0, 0, 1 - kt)
    start(pass_copy(0, 1 - kt))
    forward(1)
    step_wait(0, 1, kt)
    target_ready(2)
    step_wait(0, 1, 1 - kt)
    wait_first(1)
    step_start(1, 1)
    step_start(1, 0)
    target_ready(3)
    for cp in kernel_first:
        cp.wait_recv()
    for cp in kernel_second:
        start(cp)
    forward(2)
    forward(3)
    pass_wait(0, kt)
    target_ready(4)
    pass_wait(0, 1 - kt)
    step_wait(1, 1, kt)
    start(pass_copy(1, kt))
    target_ready(5)
    step_wait(1, 1, 1 - kt)
    start(pass_copy(1, 1 - kt))
    forward(4)
    for cp in kernel_second:
        cp.wait_recv()
    start(kernel_third)
    forward(5)
    step_wait(1, 0, kt)
    target_ready(6)
    step_wait(1, 0, 1 - kt)
    forward(6)
    kernel_third.wait_recv()
    unpack_kernel(kp, kern)
    pass_wait(1, kt)
    target_ready(7)
    pass_wait(1, 1 - kt)
    forward(7)
    middle(0, kern, fx, ix, z)
    forward(8)
    forward(9)
    forward(10)

    s_core = slots(3)
    s_result = slots(12)

    def core_sum(n):
        return remote(part.at[n, 0], rcore.at[n], s_core + n, sibling)

    def result(n, d):
        zz = (plane + d) % 4
        return remote(part.at[n, 1, zz], acc.at[n, plane], s_result + 4 * n + d, result_device(n, zz))

    result_keep = pltpu.make_async_copy(part.at[0, 1, plane], acc.at[0, plane], local.at[16])

    @pl.loop(0, 3)
    def _(u):
        n = 2 - u

        @pl.when(n > 0)
        def _():
            middle(n, kern, fx, ix, z)

        @pl.loop(0, 2)
        def _(g):
            inverse_slabs(n, (home + 1 + g) % 2, phi, iz, tw, z, s, part.at[n, g])

            @pl.when(g == 0)
            def _():
                core_sum(n).start()

        core_sum(n).wait_recv()

        @pl.loop(0, 4)
        def _(i):
            part[n, 1, i] = part[n, 1, i] + rcore[n, i]

        for d in (2, 1, 3):
            result(n, d).start()

        @pl.when(jnp.logical_or(n > 0, jnp.logical_not(mine)))
        def _():
            result(n, 0).start()

    @pl.when(mine)
    def _():
        result_keep.start()
        result_keep.wait()

    for n in (2, 1, 0):
        for d in range(4):
            if n == 0 and d == 0:

                @pl.when(jnp.logical_not(mine))
                def _():
                    result(0, 0).wait()
            else:
                result(n, d).wait()
        core_sum(n).wait_send()

    @pl.loop(0, 4)
    def _(i):
        out[i] = acc[0, i] + acc[1, i] + acc[2, i]

    for cp in sent:
        cp.wait_send()

    @pl.when(jnp.logical_not(mine))
    def _():
        for k in range(2):
            firsts[0, k].wait_send()

    @pl.when(owner)
    def _():
        for j in range(8):
            keep, give, back, beside = own_target(j)
            give.wait_send()
            back.wait_send()
            arrive, relay, give = far_target(j)
            give.wait_send()
            near_target(j)[1].wait_send()

            @pl.when(odd == 1)
            def _():
                beside.wait_send()

            @pl.when(odd == 0)
            def _():
                relay.wait_send()


def local(orbitals, kernel):
    vmem = pl.BlockSpec(memory_space=pltpu.VMEM)
    anywhere = pl.BlockSpec(memory_space=pl.ANY)
    constants = [jnp.asarray(table) for table in tables()]
    return pl.pallas_call(
        body,
        out_shape=jax.ShapeDtypeStruct(orbitals.shape, F32),
        in_specs=[anywhere] * 7,
        out_specs=vmem,
        scratch_shapes=[
            pltpu.VMEM((2, 8, 8, 4096), F32),
            pltpu.VMEM((3, 8, 8, 4096), F32),
            pltpu.VMEM((64, 8, 64), F32),
            pltpu.VMEM((4, 64, 128), F32),
            pltpu.VMEM((8, 4, 64, 128), F32),
            pltpu.VMEM((32, 64, 128), F32),
            pltpu.VMEM((3, 32, 128, 128), F32),
            pltpu.VMEM((4, 32, 8, 256), F32),
            pltpu.VMEM((3, 2, 4, 8, 4096), F32),
            pltpu.VMEM((3, 4, 8, 4096), F32),
            pltpu.VMEM((3, 4, 8, 4096), F32),
        ]
        + [pltpu.VMEM(table.shape, table.dtype) for table in constants]
        + [
            pltpu.SemaphoreType.DMA((84,)),
            pltpu.SemaphoreType.DMA((84,)),
            pltpu.SemaphoreType.DMA((17,)),
        ],
        compiler_params=pltpu.CompilerParams(
            collective_id=0, has_side_effects=True, vmem_limit_bytes=56 * 2**20
        ),
    )(orbitals, kernel, *constants)


def solution(mesh):
    return jax.shard_map(
        local,
        mesh=mesh,
        in_specs=(P("band", "grid", None), P(None, "grid", None)),
        out_specs=P("band", "grid", None),
        check_vma=False,
    )
```

profile of v0, /device:TPU:0, one launch (start us, length us, event | category | flops | bytes accessed | tf_op | source)
XLA Modules:
  0.0 79.0 jit_solution(10233557500708895480)
XLA Ops:
  0.0 77.1 %shard_map.73 = f32[4,8,4096]{2,1,0:T(8,128)} custom-call(f32[4,8,4096]{2,1,0:T(8,128)} %orb.1, f32[64,8,64]{2,1,0:T(8,128)} %kernel.1, bf16[128,384]{1,0:T(8,128)(2,1)} %constant.10.clone.fx_in, bf16[128,384]{1,0:T(8,128)(2,1)} %constant.11.clone.ix_in, bf16[768,256]{1,0:T(8,128)(2,1)} %constant.12.clone.fz_in, bf16[768,256]{1,0:T(8,128)(2,1)} %constant.13.clone.iz_in, ...), custom_call_target="tpu_custom_call" | custom-call | tf_op jit(solution)/shard_map/pallas_call | solution.py:599
  77.1 1.9 %copy.9 = f32[4,8,4096]{2,1,0:T(8,128)} copy(f32[4,8,4096]{2,1,0:T(8,128)} %shard_map.73) | data formatting | bytes 1048576
where the time goes:
time: 79.1 us; the launch traced here: 79 us
  Pallas kernels  77.1 us (97%)
  local copies, waits for them, and re-layouts  1.87 us (2%)
    pallas_call x1, Pallas kernels, local(): pl.pallas_call(body, out_shape=jax.ShapeDtypeStruct(orbitals.shape, F32),...  77.1 us
    unnamed x1, local copies, waits for them, and re-layouts  1.87 us

commit v1 on v0

--- a/solution.py
+++ b/solution.py
@@ -15,6 +15,7 @@
 H = math.sqrt(0.5)
 MESH = pl.DeviceIdType.MESH
 YA = 16
+RELAYED = (0, 1, 2, 3, 4, 5, 6, 7)
 
 
 def split_table(matrix):
@@ -168,7 +169,7 @@
         im = z[n, :, pl.ds(64 + base, 8), :].reshape(256, 128)
         rows.append(jnp.concatenate([re, im], 1))
     hi, lo = split(jnp.concatenate(rows, 0))
-    s[...] = dot(jnp.concatenate([hi, lo, hi], 1), iz[...]).reshape(4, 32, 8, 256)
+    s[0:4] = dot(jnp.concatenate([hi, lo, hi], 1), iz[...]).reshape(4, 32, 8, 256)
 
     @pl.loop(0, 4)
     def _(zz):
@@ -200,29 +201,46 @@
 
 def body(
     orb, kernel, fx_in, ix_in, fz_in, iz_in, tw_in, out,
-    phi, targ, kslab, kpk, kp, kern, z, s, part, rcore, acc, fx, ix, fz, iz, tw, send, recv, local,
+    phi, targ, kslab, kpk, kp, kern, z, s, part, rcore, acc, extra, fx, ix, fz, iz, tw, send, recv, local,
 ):
     b = lax.axis_index("band")
     q = lax.axis_index("grid")
-    core, block, x = b % 2, b // 2, b // 4
-    plane, ylo = q // 2, q % 2
-    odd = (ylo + block) % 2
-    home = (core + block) % 2
+
+    def mod(value, n):
+        return lax.rem(value, jnp.int32(n))
+
+    def div(value, n):
+        return lax.div(value, jnp.int32(n))
+
+    core, block, x = mod(b, 2), div(b, 2), div(b, 4)
+    plane, ylo = div(q, 2), mod(q, 2)
+    odd = mod(ylo + block, 2)
+    home = mod(core + block, 2)
     chip = block * 2 + odd
     sibling = (block * 2 + 1 - core, q)
     near = (b, plane * 2 + 1 - ylo)
     mine = core == odd
-    owner = core == plane // 2
+    owner = core == div(plane, 2)
+    planes = [plane] + [mod(plane + d, 4) for d in (1, 2, 3)]
+    parities = [ylo, 1 - ylo]
+    slabs = [[2 * zz + p for p in parities] for zz in planes]
+    targets_here = [div(zz, 2) == core for zz in planes]
+    kt = mod(plane, 2)
+    other = 1 - kt
+    band_of = [kt, other, kt, other]
+    across = [(b, 2 * zz + ylo) for zz in planes]
+    near_slabs = [[2 * zz + mod(ylo + 1 - odd + i, 2) for i in range(2)] for zz in planes]
 
     def device(h, c, zz):
-        h = (h + 16) % 16
-        return ((h // 2) * 2 + c, zz * 2 + (h + h // 2) % 2)
+        h = mod(h + 16, 16)
+        half = div(h, 2)
+        return (half * 2 + c, zz * 2 + mod(h + half, 2))
 
     def at_plane(d):
-        return (b, ((plane + d) % 4) * 2 + ylo)
+        return across[d]
 
     def result_device(n, zz):
-        return ((chip + n) % 16, zz * 2 + home)
+        return (mod(chip + n, 16), zz * 2 + home)
 
     count = [0]
 
@@ -256,16 +274,17 @@
     for dc in range(2):
         for dq in range(8):
             if dc or dq:
-                greeted.append(((b + dc) % 2 + block * 2, (q + dq) % 8))
-    greeted.append(device(chip - 2, core, plane))
-    greeted.append(device(chip + 2, core, plane))
+                greeted.append((mod(b + dc, 2) + block * 2, mod(q + dq, 8)))
+    for dh in (-2, -1, 1, 2):
+        greeted.append(device(chip + dh, core, plane))
     for n in (1, 2):
+        behind = mod(b - n + 16, 16)
+        behind_core = mod(ylo + div(behind, 2), 2)
         for zz in range(4):
             greeted.append(result_device(n, zz))
-            behind = (b - n + 16) % 16
-            greeted.append(device(behind, (ylo + behind // 2) % 2, zz))
+            greeted.append(device(behind, behind_core, zz))
     for dx in (4, 8, 12):
-        greeted.append(((b + dx) % 16, q))
+        greeted.append((mod(b + dx, 16), q))
     for where in greeted:
         pl.semaphore_signal(barrier, inc=1, device_id=where, device_id_type=MESH)
     pl.semaphore_wait(barrier, len(greeted))
@@ -274,9 +293,22 @@
     firsts = {}
     for k in range(2):
         for dc in range(2):
-            c = (core + dc) % 2
+            c = (core, 1 - core)[dc]
             src, dst = orb.at[2 * c + k], phi.at[k, q]
             firsts[dc, k] = remote(src, dst, s_first + 2 * dc + k, (block * 2 + c, plane * 2 + home), s_first + 2 * ylo + k)
+    s_direct = slots(6)
+
+    def direct(d):
+        k = planes[d]
+        slot = s_direct + 2 * d - 2
+        return remote(orb.at[k], phi.at[band_of[d], q], slot, (block * 2 + div(k, 2), k * 2 + home), slot + ylo)
+
+    def direct_wait(d, i):
+        piece = phi.at[kt, slabs[d][i]]
+        remote(piece, piece, s_direct, (b, q), s_direct + 2 * (4 - d) - 2 + parities[i]).wait_recv()
+
+    for d in (1, 3, 2):
+        start(direct(d))
     keeps = [pltpu.make_async_copy(orb.at[2 * core + k], phi.at[k, q], local.at[6 + k]) for k in range(2)]
     for k in range(2):
 
@@ -291,9 +323,9 @@
         start(firsts[1, k])
 
     def wait_first(i):
-        p = (ylo + i) % 2
+        p = parities[i]
         for k in range(2):
-            piece = phi.at[k, 2 * plane + p]
+            piece = phi.at[k, slabs[0][i]]
             cp = remote(piece, piece, s_first, (b, q), s_first + 2 * p + k)
             if i == 0:
 
@@ -311,29 +343,49 @@
     s_pass = slots(4)
 
     def slab_at(d, i):
-        return ((plane + d) % 4) * 2 + (ylo + i) % 2
+        return slabs[d][i]
 
     def step_copy(i, side, k):
         d = (1, 3)[side]
         piece = phi.at[k, slab_at(0, i)]
         return remote(piece, piece, s_step + 4 * i + 2 * side + k, at_plane(d))
 
+    def start_it(cp):
+        cp.start()
+
+    def wait_sent(cp):
+        cp.wait_send()
+
     def step_wait(i, side, k):
         piece = phi.at[k, slab_at((3, 1)[side], i)]
         remote(piece, piece, s_step, (b, q), s_step + 4 * i + 2 * side + k).wait_recv()
 
-    def pass_copy(i, k):
-        piece = phi.at[k, slab_at((3, 1)[i], i)]
-        return remote(piece, piece, s_pass + 2 * i + k, at_plane((1, 3)[i]))
+    def pass_copy(i, which):
+        side = (i + which) % 2
+        piece = phi.at[band_of[which], slab_at((3, 1)[side], i)]
+        return remote(piece, piece, s_pass + 2 * i + which, at_plane((1, 3)[side]), s_pass + 2 * i + band_of[which])
 
     def pass_wait(i, k):
         piece = phi.at[k, slab_at(2, i)]
         remote(piece, piece, s_pass, (b, q), s_pass + 2 * i + k).wait_recv()
 
-    def step_start(i, side):
-        d = (1, 3)[side]
-        for turn in range(2):
-            start(step_copy(i, side, (plane + d + turn) % 2))
+    def unless(condition):
+        return pl.when(jnp.logical_not(condition))
+
+    def each_other(i, act):
+        for side, d in enumerate((1, 3)):
+            act(step_copy(i, side, kt))
+
+            @unless(targets_here[d])
+            def _():
+                act(step_copy(i, side, other))
+
+    def each_pass(i, act):
+        act(pass_copy(i, 0))
+
+        @unless(targets_here[(3, 1)[i]])
+        def _():
+            act(pass_copy(i, 1))
 
     s_t0 = slots(8)
     s_t1 = slots(8)
@@ -341,13 +393,12 @@
     s_t1_give = slots(8)
     s_t2_give = slots(8)
     order = [(0, 0), (3, 0), (1, 0), (0, 1), (2, 0), (1, 1), (3, 1), (2, 1)]
-    kt = plane % 2
     far_back = device(chip - 2, core, plane)
+    near_back = device(chip - 1, core, plane)
 
     def target_slab(n, j):
         d, i = order[j]
-        flip = (0, 1 - odd, 1)[n]
-        return ((plane + d) % 4) * 2 + (ylo + flip + i) % 2
+        return (slabs[d][i], near_slabs[d][i], slabs[d][1 - i])[n]
 
     def own_target(j):
         s = target_slab(0, j)
@@ -355,7 +406,7 @@
         keep = pltpu.make_async_copy(src, targ.at[0, s], local.at[8 + j])
         give = remote(src, targ.at[0, s], s_t0 + j, sibling)
         back = remote(src, targ.at[2, s], s_t2 + j, far_back)
-        beside = remote(src, targ.at[1, s], s_t1 + j, near)
+        beside = remote(src, targ.at[1, s], s_t1 + j, near_back)
         return keep, give, back, beside
 
     def target_ready(j):
@@ -363,11 +414,13 @@
         def _():
             keep, give, back, beside = own_target(j)
             back.start()
-
-            @pl.when(odd == 1)
-            def _():
+            if j in RELAYED:
+
+                @pl.when(odd == 1)
+                def _():
+                    beside.start()
+            else:
                 beside.start()
-
             give.start()
             keep.start()
 
@@ -375,19 +428,20 @@
         s = target_slab(2, j)
         piece = targ.at[2, s]
         arrive = remote(piece, piece, s_t2, (b, q), s_t2 + j)
-        beside = remote(piece, targ.at[1, s], s_t1 + j, near)
+        relay = remote(piece, targ.at[1, s], s_t1 + j, near)
         give = remote(piece, piece, s_t2_give + j, sibling)
-        return arrive, beside, give
+        return arrive, relay, give
 
     def far_ready(j):
         @pl.when(owner)
         def _():
-            arrive, beside, give = far_target(j)
+            arrive, relay, give = far_target(j)
             arrive.wait_recv()
-
-            @pl.when(odd == 0)
-            def _():
-                beside.start()
+            if j in RELAYED:
+
+                @pl.when(odd == 0)
+                def _():
+                    relay.start()
 
             give.start()
 
@@ -419,90 +473,90 @@
     s_kernel = slots(11)
     kx_half = pl.ds(pl.multiple_of(32 * core, 32), 32)
     kernel_first = [
-        remote(kpk.at[x, kx_half], kp.at[q, x, kx_half], s_kernel + d - 1, (b, (q + d) % 8)) for d in range(1, 8)
+        remote(kpk.at[x, kx_half], kp.at[q, x, kx_half], s_kernel + d - 1, (b, mod(q + d, 8))) for d in range(1, 8)
     ]
     kernel_second = [
-        remote(kp.at[:, x, kx_half], kp.at[:, x, kx_half], s_kernel + 6 + d, ((b + 4 * d) % 16, q)) for d in (1, 3, 2)
+        remote(kp.at[:, x, kx_half], kp.at[:, x, kx_half], s_kernel + 6 + d, (mod(b + 4 * d, 16), q)) for d in (1, 3, 2)
     ]
     kernel_third = remote(kp.at[:, :, kx_half], kp.at[:, :, kx_half], s_kernel + 10, sibling)
 
     def pack_kernel():
-        loads[0].wait()
         for r in range(4):
             kpk[r] = jnp.concatenate([kslab[:, r, :], kslab[:, r + 4, :]], 1)
         for cp in kernel_first:
             start(cp)
         kp[q, x, kx_half] = kpk[x, kx_half]
 
-    far_steps = {3: (0,), 5: (2, 3), 6: (1,), 7: (4, 5), 8: (6,), 9: (7,)}
-    near_steps = {3: (0,), 5: (2,), 6: (1, 3), 7: (4,), 8: (5,), 9: (6,), 10: (7,)}
-
-    def forward(j):
-        if 2 <= j < 10:
-            far_ready(j - 2)
-        if 3 <= j < 11:
-            near_ready(j - 3)
-        active = [(0, j)] if j < 8 else []
-        active += [(2, i) for i in far_steps.get(j, ())] + [(1, i) for i in near_steps.get(j, ())]
-        for n, i in active:
-            wait_target(n, i)
-        active = [(n, target_slab(n, i)) for n, i in active]
-        forward_slabs(active, targ, phi, fz, tw, z, s)
+    def forward(*active):
+        for n, j in active:
+            wait_target(n, j)
+        forward_slabs([(n, target_slab(n, j)) for n, j in active], targ, phi, fz, tw, z, s)
+
+    def near_others(i, side):
+        step_wait(i, side, other)
+
+        @unless(owner)
+        def _():
+            step_wait(i, side, kt)
+
+    def far_others(i):
+        pass_wait(i, other)
+
+        @unless(owner)
+        def _():
+            pass_wait(i, kt)
+
+    def target_here(j):
+        @pl.when(owner)
+        def _():
+            direct_wait(*order[j])
+
+        target_ready(j)
 
     wait_first(0)
-    step_start(0, 0)
-    step_start(0, 1)
+    each_other(0, start_it)
     target_ready(0)
+    target_here(1)
+    target_here(2)
+    loads[0].wait()
     pack_kernel()
+    target_here(4)
+    target_here(5)
+    target_here(6)
     for cp in loads[1:]:
         cp.wait()
-    forward(0)
-    step_wait(0, 0, kt)
-    start(pass_copy(0, kt))
-    target_ready(1)
-    step_wait(0, 0, 1 - kt)
-    start(pass_copy(0, 1 - kt))
-    forward(1)
-    step_wait(0, 1, kt)
-    target_ready(2)
-    step_wait(0, 1, 1 - kt)
+    forward((0, 0))
+    near_others(0, 0)
+    near_others(0, 1)
+    each_pass(0, start_it)
+    target_here(7)
     wait_first(1)
-    step_start(1, 1)
-    step_start(1, 0)
+    each_other(1, start_it)
     target_ready(3)
+    far_ready(0)
+    forward((0, 1), (0, 2))
+    for j in (1, 2, 5, 6, 4):
+        far_ready(j)
+    forward((0, 3))
     for cp in kernel_first:
         cp.wait_recv()
     for cp in kernel_second:
         start(cp)
-    forward(2)
-    forward(3)
-    pass_wait(0, kt)
-    target_ready(4)
-    pass_wait(0, 1 - kt)
-    step_wait(1, 1, kt)
-    start(pass_copy(1, kt))
-    target_ready(5)
-    step_wait(1, 1, 1 - kt)
-    start(pass_copy(1, 1 - kt))
-    forward(4)
+    far_ready(7)
+    near_others(1, 1)
+    near_others(1, 0)
+    each_pass(1, start_it)
+    far_ready(3)
+    far_others(0)
+    forward((0, 4), (2, 5), (2, 6), (2, 3))
     for cp in kernel_second:
         cp.wait_recv()
     start(kernel_third)
-    forward(5)
-    step_wait(1, 0, kt)
-    target_ready(6)
-    step_wait(1, 0, 1 - kt)
-    forward(6)
+    forward((0, 5), (0, 6), (2, 7))
     kernel_third.wait_recv()
     unpack_kernel(kp, kern)
-    pass_wait(1, kt)
-    target_ready(7)
-    pass_wait(1, 1 - kt)
-    forward(7)
-    middle(0, kern, fx, ix, z)
-    forward(8)
-    forward(9)
-    forward(10)
+    far_others(1)
+    forward((0, 7))
 
     s_core = slots(3)
     s_result = slots(12)
@@ -511,22 +565,39 @@
         return remote(part.at[n, 0], rcore.at[n], s_core + n, sibling)
 
     def result(n, d):
-        zz = (plane + d) % 4
+        zz = planes[d]
         return remote(part.at[n, 1, zz], acc.at[n, plane], s_result + 4 * n + d, result_device(n, zz))
+
+    s_extra = slots(4)
+    adds = jnp.logical_and(odd == 0, core == 1)
+    gives = jnp.logical_and(odd == 1, core == 1)
+    has_near = jnp.logical_or(odd == 1, core == 1)
+
+    def exchange(d):
+        return remote(part.at[1, 1, planes[d]], extra.at[planes[d]], s_extra + d, near)
 
     result_keep = pltpu.make_async_copy(part.at[0, 1, plane], acc.at[0, plane], local.at[16])
 
     @pl.loop(0, 3)
     def _(u):
-        n = 2 - u
-
-        @pl.when(n > 0)
-        def _():
-            middle(n, kern, fx, ix, z)
+        n = mod(2 * u, 3)
+
+        @pl.when(u == 1)
+        def _():
+            for j in range(8):
+                near_ready(j)
+            forward((2, 0), (2, 1), (2, 2), (2, 4))
+
+        @pl.when(u == 2)
+        def _():
+            for j in (0, 4):
+                forward((1, j), (1, j + 1), (1, j + 2), (1, j + 3))
+
+        middle(n, kern, fx, ix, z)
 
         @pl.loop(0, 2)
         def _(g):
-            inverse_slabs(n, (home + 1 + g) % 2, phi, iz, tw, z, s, part.at[n, g])
+            inverse_slabs(n, mod(home + 1 + g, 2), phi, iz, tw, z, s, part.at[n, g])
 
             @pl.when(g == 0)
             def _():
@@ -538,35 +609,75 @@
         def _(i):
             part[n, 1, i] = part[n, 1, i] + rcore[n, i]
 
-        for d in (2, 1, 3):
-            result(n, d).start()
-
-        @pl.when(jnp.logical_or(n > 0, jnp.logical_not(mine)))
+        held = jnp.logical_or(jnp.logical_and(adds, n == 2), jnp.logical_and(gives, n == 1))
+
+        @unless(held)
+        def _():
+            for d in (2, 1, 3):
+                result(n, d).start()
+
+        @unless(jnp.logical_or(held, jnp.logical_and(n == 0, mine)))
         def _():
             result(n, 0).start()
+
+        @pl.when(jnp.logical_and(gives, n == 1))
+        def _():
+            for d in (2, 1, 3, 0):
+                exchange(d).start()
+
+    @pl.when(adds)
+    def _():
+        for d in (2, 1, 3, 0):
+            exchange(d).wait_recv()
+            part[2, 1, planes[d]] = part[2, 1, planes[d]] + extra[planes[d]]
+            result(2, d).start()
 
     @pl.when(mine)
     def _():
         result_keep.start()
         result_keep.wait()
 
-    for n in (2, 1, 0):
+    for n in range(3):
+        core_sum(n).wait_send()
+    for d in range(4):
+        result(2, d).wait()
+        if d:
+            result(0, d).wait()
+
+    @unless(mine)
+    def _():
+        result(0, 0).wait()
+
+    @pl.when(gives)
+    def _():
         for d in range(4):
-            if n == 0 and d == 0:
-
-                @pl.when(jnp.logical_not(mine))
-                def _():
-                    result(0, 0).wait()
-            else:
-                result(n, d).wait()
-        core_sum(n).wait_send()
-
-    @pl.loop(0, 4)
-    def _(i):
-        out[i] = acc[0, i] + acc[1, i] + acc[2, i]
+            exchange(d).wait_send()
+
+    @unless(gives)
+    def _():
+        for d in range(4):
+            result(1, d).wait_send()
+
+    @pl.when(has_near)
+    def _():
+        for d in range(4):
+            result(1, d).wait_recv()
+
+        @pl.loop(0, 4)
+        def _(i):
+            out[i] = acc[0, i] + acc[1, i] + acc[2, i]
+
+    @unless(has_near)
+    def _():
+        @pl.loop(0, 4)
+        def _(i):
+            out[i] = acc[0, i] + acc[2, i]
 
     for cp in sent:
         cp.wait_send()
+    for i in range(2):
+        each_other(i, wait_sent)
+        each_pass(i, wait_sent)
 
     @pl.when(jnp.logical_not(mine))
     def _():
@@ -579,17 +690,20 @@
             keep, give, back, beside = own_target(j)
             give.wait_send()
             back.wait_send()
-            arrive, relay, give = far_target(j)
-            give.wait_send()
+            arrive, relay, pass_on = far_target(j)
+            pass_on.wait_send()
+            if j in RELAYED:
+
+                @pl.when(odd == 1)
+                def _():
+                    beside.wait_send()
+
+                @pl.when(odd == 0)
+                def _():
+                    relay.wait_send()
+            else:
+                beside.wait_send()
             near_target(j)[1].wait_send()
-
-            @pl.when(odd == 1)
-            def _():
-                beside.wait_send()
-
-            @pl.when(odd == 0)
-            def _():
-                relay.wait_send()
 
 
 def local(orbitals, kernel):
@@ -609,15 +723,16 @@
             pltpu.VMEM((8, 4, 64, 128), F32),
             pltpu.VMEM((32, 64, 128), F32),
             pltpu.VMEM((3, 32, 128, 128), F32),
-            pltpu.VMEM((4, 32, 8, 256), F32),
+            pltpu.VMEM((5, 32, 8, 256), F32),
             pltpu.VMEM((3, 2, 4, 8, 4096), F32),
             pltpu.VMEM((3, 4, 8, 4096), F32),
             pltpu.VMEM((3, 4, 8, 4096), F32),
+            pltpu.VMEM((4, 8, 4096), F32),
         ]
         + [pltpu.VMEM(table.shape, table.dtype) for table in constants]
         + [
-            pltpu.SemaphoreType.DMA((84,)),
-            pltpu.SemaphoreType.DMA((84,)),
+            pltpu.SemaphoreType.DMA((92,)),
+            pltpu.SemaphoreType.DMA((92,)),
             pltpu.SemaphoreType.DMA((17,)),
         ],
         compiler_params=pltpu.CompilerParams(

time: 79.1 us -> 73.7 us (0.932)
  Pallas kernels: 77.1 us -> 71.7 us
    pallas_call x1, Pallas kernels: 77.1 us -> 71.7 us  [local(): pl.pallas_call(body, out_shape=jax.ShapeDtypeStruct(orbitals.shape, F32),...]
where the time goes in v1:
time: 73.7 us; the launch traced here: 73.5 us
  Pallas kernels  71.7 us (97%)
  local copies, waits for them, and re-layouts  1.87 us (3%)
    pallas_call x1, Pallas kernels, local(): pl.pallas_call(body, out_shape=jax.ShapeDtypeStruct(orbitals.shape, F32),...  71.7 us
    unnamed x1, local copies, waits for them, and re-layouts  1.87 us

profile of v1, /device:TPU:0, one launch (start us, length us, event | category | flops | bytes accessed | tf_op | source)
XLA Modules:
  0.0 73.5 jit_solution(15984676630645757526)
XLA Ops:
  0.0 71.7 %shard_map.73 = f32[4,8,4096]{2,1,0:T(8,128)} custom-call(f32[4,8,4096]{2,1,0:T(8,128)} %orb.1, f32[64,8,64]{2,1,0:T(8,128)} %kernel.1, bf16[128,384]{1,0:T(8,128)(2,1)} %constant.10.clone.fx_in, bf16[128,384]{1,0:T(8,128)(2,1)} %constant.11.clone.ix_in, bf16[768,256]{1,0:T(8,128)(2,1)} %constant.12.clone.fz_in, bf16[768,256]{1,0:T(8,128)(2,1)} %constant.13.clone.iz_in, ...), custom_call_target="tpu_custom_call" | custom-call | tf_op jit(solution)/shard_map/pallas_call | solution.py:713
  71.7 1.9 %copy.9 = f32[4,8,4096]{2,1,0:T(8,128)} copy(f32[4,8,4096]{2,1,0:T(8,128)} %shard_map.73) | data formatting | bytes 1048576

commit v2 on v1

--- a/solution.py
+++ b/solution.py
@@ -14,7 +14,7 @@
 F32 = jnp.float32
 H = math.sqrt(0.5)
 MESH = pl.DeviceIdType.MESH
-YA = 16
+YA = 32
 RELAYED = (0, 1, 2, 3, 4, 5, 6, 7)
 
 
@@ -578,6 +578,29 @@
 
     result_keep = pltpu.make_async_copy(part.at[0, 1, plane], acc.at[0, plane], local.at[16])
 
+    def finish(n):
+        core_sum(n).wait_recv()
+
+        @pl.loop(0, 4)
+        def _(i):
+            part[n, 1, i] = part[n, 1, i] + rcore[n, i]
+
+        held = jnp.logical_or(jnp.logical_and(adds, n == 2), jnp.logical_and(gives, n == 1))
+
+        @unless(held)
+        def _():
+            for d in (2, 1, 3):
+                result(n, d).start()
+
+        @unless(jnp.logical_or(held, jnp.logical_and(n == 0, mine)))
+        def _():
+            result(n, 0).start()
+
+        @pl.when(jnp.logical_and(gives, n == 1))
+        def _():
+            for d in (2, 1, 3, 0):
+                exchange(d).start()
+
     @pl.loop(0, 3)
     def _(u):
         n = mod(2 * u, 3)
@@ -595,35 +618,20 @@
 
         middle(n, kern, fx, ix, z)
 
+        last = div(u, 2)
+
         @pl.loop(0, 2)
         def _(g):
-            inverse_slabs(n, mod(home + 1 + g, 2), phi, iz, tw, z, s, part.at[n, g])
-
-            @pl.when(g == 0)
+            place = mod(g + core * last, 2)
+            inverse_slabs(n, mod(home + 1 + g + core * last, 2), phi, iz, tw, z, s, part.at[n, place])
+
+            @pl.when(place == 0)
             def _():
                 core_sum(n).start()
 
-        core_sum(n).wait_recv()
-
-        @pl.loop(0, 4)
-        def _(i):
-            part[n, 1, i] = part[n, 1, i] + rcore[n, i]
-
-        held = jnp.logical_or(jnp.logical_and(adds, n == 2), jnp.logical_and(gives, n == 1))
-
-        @unless(held)
-        def _():
-            for d in (2, 1, 3):
-                result(n, d).start()
-
-        @unless(jnp.logical_or(held, jnp.logical_and(n == 0, mine)))
-        def _():
-            result(n, 0).start()
-
-        @pl.when(jnp.logical_and(gives, n == 1))
-        def _():
-            for d in (2, 1, 3, 0):
-                exchange(d).start()
+            @pl.when(place == 1)
+            def _():
+                finish(n)
 
     @pl.when(adds)
     def _():
@@ -712,7 +720,7 @@
     constants = [jnp.asarray(table) for table in tables()]
     return pl.pallas_call(
         body,
-        out_shape=jax.ShapeDtypeStruct(orbitals.shape, F32),
+        out_shape=pltpu.VMEM(orbitals.shape, F32),
         in_specs=[anywhere] * 7,
         out_specs=vmem,
         scratch_shapes=[

time: 73.7 us -> 71.4 us (0.969)
  Pallas kernels: 71.7 us -> 70.5 us
  local copies, waits for them, and re-layouts: 1.87 us -> 0.8 us
    pallas_call x1, Pallas kernels: 71.7 us -> 70.5 us  [local(): pl.pallas_call(body, out_shape=pltpu.VMEM(orbitals.shape, F32), in_specs=...]
    unnamed x1, local copies, waits for them, and re-layouts: 1.87 us -> 0.8 us
where the time goes in v2:
time: 71.4 us; the launch traced here: 71.3 us
  Pallas kernels  70.5 us (99%)
  local copies, waits for them, and re-layouts  0.8 us (1%)
    pallas_call x1, Pallas kernels, local(): pl.pallas_call(body, out_shape=pltpu.VMEM(orbitals.shape, F32), in_specs=...  70.5 us

profile of v2, /device:TPU:0, one launch (start us, length us, event | category | flops | bytes accessed | tf_op | source)
XLA Modules:
  0.0 71.3 jit_solution(712044747592981613)
XLA Ops:
  0.0 70.5 %shard_map.73 = f32[4,8,4096]{2,1,0:T(8,128)S(1)} custom-call(f32[4,8,4096]{2,1,0:T(8,128)} %orb.1, f32[64,8,64]{2,1,0:T(8,128)} %kernel.1, bf16[128,384]{1,0:T(8,128)(2,1)} %constant.10.clone.fx_in, bf16[128,384]{1,0:T(8,128)(2,1)} %constant.11.clone.ix_in, bf16[768,256]{1,0:T(8,128)(2,1)} %constant.12.clone.fz_in, bf16[768,256]{1,0:T(8,128)(2,1)} %constant.13.clone.iz_in, ...), custom_call_target="tpu_custom_call" | custom-call | tf_op jit(solution)/shard_map/pallas_call | solution.py:721
  70.5 0.8 %copy.9 = f32[4,8,4096]{2,1,0:T(8,128)} copy(f32[4,8,4096]{2,1,0:T(8,128)S(1)} %shard_map.73) | data formatting | bytes 1048576

commit v3 on v2

--- a/solution.py
+++ b/solution.py
@@ -111,7 +111,7 @@
     return jnp.dot(a, b, preferred_element_type=F32)
 
 
-def forward_slabs(active, targ, phi, fz, tw, z, s):
+def forward_slabs(active, targ, phi, fz, tw, z, s, apart=False):
     count = len(active)
 
     def pick(u, values):
@@ -122,11 +122,7 @@
             total = total + row[0] * (chosen // math.factorial(order))
         return total
 
-    @pl.loop(0, count)
-    def _(u):
-        n = pick(u, [n for n, _ in active])
-        slab = pick(u, [slab for _, slab in active])
-
+    def transform(u, n, slab):
         def load(y):
             at = slice(128 * y, 128 * (y + 1))
             t = targ[n, slab, :, at]
@@ -139,13 +135,27 @@
 
         dft32(load, store, -1)
 
-    hi, lo = split(s[0:count].reshape(count * 256, 256))
-    res = dot(jnp.concatenate([hi, lo, hi], 1), fz[...])
-    for u, (n, slab) in enumerate(active):
-        part = res[256 * u : 256 * (u + 1)]
-        base = pl.multiple_of(8 * slab, 8)
-        z[n, :, pl.ds(base, 8), :] = part[:, :128].reshape(32, 8, 128)
-        z[n, :, pl.ds(64 + base, 8), :] = part[:, 128:].reshape(32, 8, 128)
+    def multiply(first, last):
+        hi, lo = split(s[first:last].reshape((last - first) * 256, 256))
+        res = dot(jnp.concatenate([hi, lo, hi], 1), fz[...])
+        for u, (n, slab) in enumerate(active[first:last]):
+            part = res[256 * u : 256 * (u + 1)]
+            base = pl.multiple_of(8 * slab, 8)
+            z[n, :, pl.ds(base, 8), :] = part[:, :128].reshape(32, 8, 128)
+            z[n, :, pl.ds(64 + base, 8), :] = part[:, 128:].reshape(32, 8, 128)
+
+    if apart:
+        for u, (n, slab) in enumerate(active):
+            transform(u, n, slab)
+            if u % 2 or u == count - 1:
+                multiply(u - u % 2, u + 1)
+    else:
+
+        @pl.loop(0, count)
+        def _(u):
+            transform(u, pick(u, [n for n, _ in active]), pick(u, [slab for _, slab in active]))
+
+        multiply(0, count)
 
 
 def middle(n, kern, fx, ix, z):
@@ -169,15 +179,13 @@
         im = z[n, :, pl.ds(64 + base, 8), :].reshape(256, 128)
         rows.append(jnp.concatenate([re, im], 1))
     hi, lo = split(jnp.concatenate(rows, 0))
-    s[0:4] = dot(jnp.concatenate([hi, lo, hi], 1), iz[...]).reshape(4, 32, 8, 256)
-
-    @pl.loop(0, 4)
-    def _(zz):
+    res = dot(jnp.concatenate([hi, lo, hi], 1), iz[...]).reshape(4, 32, 8, 256)
+    for zz in range(4):
         slab = 2 * zz + parity
 
         def load(k):
             c, w = tw[k, 0], tw[k, 1]
-            r, i = s[zz, k, :, 0:128], s[zz, k, :, 128:256]
+            r, i = res[zz, k, :, 0:128], res[zz, k, :, 128:256]
             return r * c - i * w, i * c + r * w
 
         def store(y, v):
@@ -487,10 +495,10 @@
             start(cp)
         kp[q, x, kx_half] = kpk[x, kx_half]
 
-    def forward(*active):
+    def forward(*active, apart=False):
         for n, j in active:
             wait_target(n, j)
-        forward_slabs([(n, target_slab(n, j)) for n, j in active], targ, phi, fz, tw, z, s)
+        forward_slabs([(n, target_slab(n, j)) for n, j in active], targ, phi, fz, tw, z, s, apart)
 
     def near_others(i, side):
         step_wait(i, side, other)
@@ -514,8 +522,8 @@
         target_ready(j)
 
     wait_first(0)
+    target_ready(0)
     each_other(0, start_it)
-    target_ready(0)
     target_here(1)
     target_here(2)
     loads[0].wait()
@@ -531,8 +539,8 @@
     each_pass(0, start_it)
     target_here(7)
     wait_first(1)
+    target_ready(3)
     each_other(1, start_it)
-    target_ready(3)
     far_ready(0)
     forward((0, 1), (0, 2))
     for j in (1, 2, 5, 6, 4):
@@ -609,12 +617,12 @@
         def _():
             for j in range(8):
                 near_ready(j)
-            forward((2, 0), (2, 1), (2, 2), (2, 4))
+            forward((2, 0), (2, 1), (2, 2), (2, 4), apart=True)
 
         @pl.when(u == 2)
         def _():
             for j in (0, 4):
-                forward((1, j), (1, j + 1), (1, j + 2), (1, j + 3))
+                forward((1, j), (1, j + 1), (1, j + 2), (1, j + 3), apart=True)
 
         middle(n, kern, fx, ix, z)
 

time: 71.4 us -> 70.2 us (0.983)
  Pallas kernels: 70.5 us -> 69.2 us
    pallas_call x1, Pallas kernels: 70.5 us -> 69.2 us  [local(): pl.pallas_call(body, out_shape=pltpu.VMEM(orbitals.shape, F32), in_specs=...]
where the time goes in v3:
time: 70.2 us; the launch traced here: 70 us
  Pallas kernels  69.2 us (99%)
  local copies, waits for them, and re-layouts  0.8 us (1%)
    pallas_call x1, Pallas kernels, local(): pl.pallas_call(body, out_shape=pltpu.VMEM(orbitals.shape, F32), in_specs=...  69.2 us

profile of v3, /device:TPU:0, one launch (start us, length us, event | category | flops | bytes accessed | tf_op | source)
XLA Modules:
  0.0 70.0 jit_solution(16975189044930331011)
XLA Ops:
  0.0 69.2 %shard_map.73 = f32[4,8,4096]{2,1,0:T(8,128)S(1)} custom-call(f32[4,8,4096]{2,1,0:T(8,128)} %orb.1, f32[64,8,64]{2,1,0:T(8,128)} %kernel.1, bf16[128,384]{1,0:T(8,128)(2,1)} %constant.10.clone.fx_in, bf16[128,384]{1,0:T(8,128)(2,1)} %constant.11.clone.ix_in, bf16[768,256]{1,0:T(8,128)(2,1)} %constant.12.clone.fz_in, bf16[768,256]{1,0:T(8,128)(2,1)} %constant.13.clone.iz_in, ...), custom_call_target="tpu_custom_call" | custom-call | tf_op jit(solution)/shard_map/pallas_call | solution.py:729
  69.2 0.8 %copy.9 = f32[4,8,4096]{2,1,0:T(8,128)} copy(f32[4,8,4096]{2,1,0:T(8,128)S(1)} %shard_map.73) | data formatting | bytes 1048576

commit v4 on v3

--- a/solution.py
+++ b/solution.py
@@ -653,42 +653,6 @@
         result_keep.start()
         result_keep.wait()
 
-    for n in range(3):
-        core_sum(n).wait_send()
-    for d in range(4):
-        result(2, d).wait()
-        if d:
-            result(0, d).wait()
-
-    @unless(mine)
-    def _():
-        result(0, 0).wait()
-
-    @pl.when(gives)
-    def _():
-        for d in range(4):
-            exchange(d).wait_send()
-
-    @unless(gives)
-    def _():
-        for d in range(4):
-            result(1, d).wait_send()
-
-    @pl.when(has_near)
-    def _():
-        for d in range(4):
-            result(1, d).wait_recv()
-
-        @pl.loop(0, 4)
-        def _(i):
-            out[i] = acc[0, i] + acc[1, i] + acc[2, i]
-
-    @unless(has_near)
-    def _():
-        @pl.loop(0, 4)
-        def _(i):
-            out[i] = acc[0, i] + acc[2, i]
-
     for cp in sent:
         cp.wait_send()
     for i in range(2):
@@ -720,6 +684,42 @@
             else:
                 beside.wait_send()
             near_target(j)[1].wait_send()
+
+    for n in range(3):
+        core_sum(n).wait_send()
+    for d in range(4):
+        result(2, d).wait()
+        if d:
+            result(0, d).wait()
+
+    @unless(mine)
+    def _():
+        result(0, 0).wait()
+
+    @pl.when(gives)
+    def _():
+        for d in range(4):
+            exchange(d).wait_send()
+
+    @unless(gives)
+    def _():
+        for d in range(4):
+            result(1, d).wait_send()
+
+    @pl.when(has_near)
+    def _():
+        for d in range(4):
+            result(1, d).wait_recv()
+
+        @pl.loop(0, 4)
+        def _(i):
+            out[i] = acc[0, i] + acc[1, i] + acc[2, i]
+
+    @unless(has_near)
+    def _():
+        @pl.loop(0, 4)
+        def _(i):
+            out[i] = acc[0, i] + acc[2, i]
 
 
 def local(orbitals, kernel):

time: 70.2 us -> 70.1 us (level)
  no operation moved by 1% of the time
where the time goes in v4:
time: 70.1 us; the launch traced here: 69.9 us
  Pallas kernels  69.1 us (99%)
  local copies, waits for them, and re-layouts  0.8 us (1%)
    pallas_call x1, Pallas kernels, local(): pl.pallas_call(body, out_shape=pltpu.VMEM(orbitals.shape, F32), in_specs=...  69.1 us

profile of v4, /device:TPU:0, one launch (start us, length us, event | category | flops | bytes accessed | tf_op | source)
XLA Modules:
  0.0 69.9 jit_solution(4318228363969221450)
XLA Ops:
  0.0 69.1 %shard_map.73 = f32[4,8,4096]{2,1,0:T(8,128)S(1)} custom-call(f32[4,8,4096]{2,1,0:T(8,128)} %orb.1, f32[64,8,64]{2,1,0:T(8,128)} %kernel.1, bf16[128,384]{1,0:T(8,128)(2,1)} %constant.10.clone.fx_in, bf16[128,384]{1,0:T(8,128)(2,1)} %constant.11.clone.ix_in, bf16[768,256]{1,0:T(8,128)(2,1)} %constant.12.clone.fz_in, bf16[768,256]{1,0:T(8,128)(2,1)} %constant.13.clone.iz_in, ...), custom_call_target="tpu_custom_call" | custom-call | tf_op jit(solution)/shard_map/pallas_call | solution.py:729
  69.1 0.8 %copy.9 = f32[4,8,4096]{2,1,0:T(8,128)} copy(f32[4,8,4096]{2,1,0:T(8,128)S(1)} %shard_map.73) | data formatting | bytes 1048576
